TPU v7x, 1024 devices: a whole 4x4x32 slice. The times are simulated.
1024 devices in a mesh: group: 16 (over y, x_lo, core), local: 64 (over z, x_hi).
Axes of the slice: x: 4 (x_hi: 2, x_lo: 2; x = x_hi * 2 + x_lo), y: 4, z: 32, core: 2. Of those that a mesh axis runs over, the one named last changes fastest.
Arguments:
- grad_out: bfloat16 [2048, 3584], P(('group', 'local')), may hold values from -6 to 6
- routes: int32 [2048, 8], replicated, may hold values from 0 to 127, as said below
- router_weights: float32 [2048, 8], replicated, may hold values from 0.05 to 0.5
- gate_weight: bfloat16 [1024, 3584, 128], P(('group', 'local')), may hold values from -0.09375 to 0.09375
- up_weight: bfloat16 [1024, 3584, 128], P(('group', 'local')), may hold values from -0.09375 to 0.09375
- down_weight: bfloat16 [1024, 128, 3584], P(('group', 'local')), may hold values from -0.1875 to 0.1875
- saved_gate: bfloat16 [1024, 256, 128], P(('group', 'local')), may hold values from -6 to 6
- saved_up: bfloat16 [1024, 256, 128], P(('group', 'local')), may hold values from -6 to 6
Outputs:
- grad_in: bfloat16 [2048, 3584], P(('group', 'local'))
- grad_gate: bfloat16 [2048, 8], P(('group', 'local'))
Inputs may be any that keep to these rules, and one draw needn't show every extreme that they name: `routes`: each token names 8 different experts, two in each of 4 different groups. Of the tokens that share one local index, every group is named by exactly 8, and at most 4 name one expert; in every group two experts are named by exactly 4 of them for every local index.
All inputs are finite; a program needn't handle non-finite values.
Results may differ from a plain program's by a relative error of at most 0.0075.
Values may be sent and summed in bfloat16 or wider, within the bound.
A program may use at most 32 MiB of HBM per device.

v0:
```python
import jax
import jax.numpy as jnp
from jax import lax
from jax.sharding import PartitionSpec as P

EXP_GROUP = 8
TOPG = 4


def expert_backward(expert_rows, w_gate, w_up, w_down, pre_gate, pre_up):
    contract = (((1,), (1,)), ((), ()))
    act_grad = lax.dot_general(expert_rows, w_down, contract, preferred_element_type=jnp.float32)
    gate_val = pre_gate.astype(jnp.float32)
    up_projection_value = pre_up.astype(jnp.float32)
    sigma = jax.nn.sigmoid(gate_val)
    active = gate_val * sigma
    gate_part = jnp.sum(active * up_projection_value * act_grad, axis=1).astype(jnp.bfloat16)
    grad_gate_pre = (
        act_grad * up_projection_value * sigma * (1.0 + gate_val * (1.0 - sigma))
    ).astype(jnp.bfloat16)
    grad_up_pre = (act_grad * active).astype(jnp.bfloat16)
    partial_in = lax.dot_general(
        grad_gate_pre, w_gate, contract, preferred_element_type=jnp.float32
    )
    partial_in = partial_in + lax.dot_general(
        grad_up_pre, w_up, contract, preferred_element_type=jnp.float32
    )
    return (partial_in.astype(jnp.bfloat16), gate_part)


def slot_tables(route_column, expert, capacity):
    named_route = route_column == expert
    is_named = jnp.any(named_route, axis=1)
    slot_order = jnp.cumsum(is_named.astype(jnp.int32)) - 1
    slot_ids = jnp.arange(capacity, dtype=jnp.int32)
    onehot = is_named[None, :] & (slot_order[None, :] == slot_ids[:, None])
    return (onehot.astype(jnp.float32), named_route.astype(jnp.float32))


def local(
    grad_out, routes, router_weights, gate_weight, up_weight, down_weight, saved_gate, saved_up
):
    n_group = lax.axis_size("group")
    n_local = lax.axis_size("local")
    group_index = lax.axis_index("group")
    resident_index = lax.axis_index("local")
    tok_dev = grad_out.shape[0]
    model_width = grad_out.shape[1]
    route_count = routes.shape[1]
    n_split = n_local // EXP_GROUP
    column = n_group * tok_dev
    capacity = TOPG * tok_dev // 2
    live_count = TOPG * tok_dev
    highest = lax.Precision.HIGHEST

    def by_column(table):
        return jnp.swapaxes(table.reshape(n_group, n_local, tok_dev, route_count), 0, 1).reshape(
            n_local, column, route_count
        )

    route_columns = by_column(routes)
    weight_cols = by_column(router_weights)
    own_routes = lax.dynamic_index_in_dim(route_columns, resident_index, 0, keepdims=False)
    own_weights = lax.dynamic_index_in_dim(weight_cols, resident_index, 0, keepdims=False)
    grad_rows = lax.all_gather(grad_out, "group", axis=0, tiled=True)
    group_experts = group_index * EXP_GROUP + jnp.arange(EXP_GROUP, dtype=jnp.int32)
    group_onehot, group_named = jax.vmap(lambda expert: slot_tables(own_routes, expert, capacity))(
        group_experts
    )

    def packed_order(route_column):
        in_group = jnp.any(route_column // EXP_GROUP == group_index, axis=1)
        position = jnp.cumsum(in_group.astype(jnp.int32)) - 1
        live_ids = jnp.arange(live_count, dtype=jnp.int32)
        return (in_group[None, :] & (position[None, :] == live_ids[:, None])).astype(jnp.float32)

    selected_routes = jax.vmap(packed_order)(route_columns)
    own_pick = lax.dynamic_index_in_dim(selected_routes, resident_index, 0, keepdims=False)
    compact = jnp.dot(
        own_pick.astype(jnp.bfloat16), grad_rows, preferred_element_type=jnp.float32
    ).astype(jnp.bfloat16)
    gathered = lax.all_gather(compact, "local", axis=0, tiled=True).reshape(
        n_local, live_count, model_width
    )
    my_expert = group_index * EXP_GROUP + resident_index // n_split
    mine_onehot, mine_named = jax.vmap(
        lambda route_column: slot_tables(route_column, my_expert, capacity)
    )(route_columns)
    slot_matrix = jnp.einsum("scr,sjr->scj", mine_onehot, selected_routes).astype(jnp.bfloat16)
    expert_rows = jnp.einsum(
        "scj,sjf->scf", slot_matrix, gathered, preferred_element_type=jnp.float32
    ).astype(jnp.bfloat16)
    expert_rows = expert_rows.reshape(n_local * capacity, model_width)
    partial_in, gate_part = expert_backward(
        expert_rows, gate_weight[0], up_weight[0], down_weight[0], saved_gate[0], saved_up[0]
    )
    returned, gate_back = (
        lax.all_to_all(
            partial_in.reshape(n_local, capacity, model_width),
            "local",
            split_axis=0,
            concat_axis=0,
            tiled=True,
        ),
        lax.all_to_all(
            gate_part.reshape(n_local, capacity), "local", split_axis=0, concat_axis=0, tiled=True
        ),
    )
    slice_sums = jnp.sum(
        returned.reshape(EXP_GROUP, n_split, capacity, model_width), axis=1, dtype=jnp.float32
    )
    gate_sums = jnp.sum(gate_back.reshape(EXP_GROUP, n_split, capacity), axis=1, dtype=jnp.float32)
    route_weight = jnp.sum(group_named * own_weights[None], axis=2)
    group_sum = jnp.einsum(
        "xcr,xcf->rf", group_onehot * route_weight[:, None, :], slice_sums, precision=highest
    ).astype(jnp.bfloat16)
    gate_sum = jnp.einsum(
        "xcr,xrk,xc->rk", group_onehot, group_named, gate_sums, precision=highest
    ).astype(jnp.bfloat16)
    arrived, gate_arrived = (
        lax.all_to_all(
            group_sum.reshape(n_group, tok_dev, model_width),
            "group",
            split_axis=0,
            concat_axis=0,
            tiled=True,
        ),
        lax.all_to_all(
            gate_sum.reshape(n_group, tok_dev, route_count),
            "group",
            split_axis=0,
            concat_axis=0,
            tiled=True,
        ),
    )
    grad_in = jnp.sum(arrived, axis=0, dtype=jnp.float32).astype(jnp.bfloat16)
    grad_gate = jnp.sum(gate_arrived, axis=0, dtype=jnp.float32).astype(jnp.bfloat16)
    return (grad_in, grad_gate)


def solution(mesh):
    placed = (
        P(("group", "local"), None),
        P(),
        P(),
        P(("group", "local"), None, None),
        P(("group", "local"), None, None),
        P(("group", "local"), None, None),
        P(("group", "local"), None, None),
        P(("group", "local"), None, None),
    )
    return jax.shard_map(
        local,
        mesh=mesh,
        in_specs=placed,
        out_specs=(P(("group", "local"), None), P(("group", "local"), None)),
        check_vma=False,
    )
```

profile of v0, /device:TPU:1, one launch (start us, length us, event | category | flops | bytes accessed | tf_op | source)
XLA Modules:
  0.0 604.5 jit_solution(14535403447282061303)
XLA Ops:
  7.3 1.2 copy.70
  8.5 34.8 %compare_reduce_fusion.1 = (pred[64,16,2]{2,0,1:T(8,128)(4,1)S(1)}, pred[64,16,2]{2,0,1:T(8,128)(4,1)S(1)}) fusion(s32[64,16,2,8]{3,2,0,1:T(2,128)S(1)} %bitcast.76, s32[]{:T(128)S(6)} %add.51, s32[]{:T(128)S(6)} %axis_index.25), kind=kLoop, calls=%fused_computation.10 | loop fusion | flops 307200 | bytes 69640 | tf_op jit(solution)/shard_map/vmap()/reduce_or | solution.py:33
  43.4 0.2 copy.79
  43.6 0.1 copy.80
  43.8 31.4 %all-gather = bf16[16,2,3584]{2,1,0:T(2,128)(2,1)S(1)} all-gather(bf16[1,2,3584]{2,1,0:T(2,128)(2,1)} %bitcast.86), channel_id=1, replica_groups=mesh['group'=16,'local'=64] {'group'}, dimensions={0}, use_global_device_ids=true | all-gather | bytes 243712 | tf_op jit(solution)/shard_map/all_gather | solution.py:65
  75.1 0.1 reshape.115
  75.2 0.1 copy.81
  75.3 0.2 reduce_window_sum.30
  75.6 0.8 convolution_convert_fusion.1
  76.4 0.2 copy.76
  76.6 0.1 copy.77
  76.8 0.1 copy.83
  76.9 0.1 copy.82
  77.0 0.1 copy.78
  77.1 0.2 reduce_window_sum.29
  77.3 263.6 %all-gather.3.cloned.1.call-done = bf16[512,3584]{1,0:T(8,128)(2,1)} async-done(((bf16[8,3584]{1,0:T(8,128)(2,1)}), bf16[512,3584]{1,0:T(8,128)(2,1)}) %all-gather.3.cloned.1.call-update) | async-done | bytes 3670032 | tf_op jit(solution)/shard_map/all_gather | solution.py:82
  340.9 4.5 convolution_convert_fusion
  345.4 4.0 reshape.106
  349.4 2.5 fusion.14
  351.9 0.7 convert_element_type.130
  352.6 13.3 %all-to-all-start.2 = ((bf16[64,1,4]{2,1,0:T(2,128)(2,1)}), bf16[64,1,4]{2,1,0:T(2,128)(2,1)S(1)}, u32[]{:S(2)}, u32[]{:S(2)}) async-start(bf16[64,1,4]{2,1,0:T(2,128)(2,1)} %convert_element_type.130), calls=%async_computation.2 | async-start | bytes 65536 | tf_op jit(solution)/shard_map/all_to_all | solution.py:105
  366.0 0.7 fusion.4
  366.7 1.9 fusion
  368.6 4.1 reshape.107
  372.7 16.8 %all-to-all-done.2 = bf16[64,1,4]{2,1,0:T(2,128)(2,1)S(1)} async-done(((bf16[64,1,4]{2,1,0:T(2,128)(2,1)}), bf16[64,1,4]{2,1,0:T(2,128)(2,1)S(1)}, u32[]{:S(2)}, u32[]{:S(2)}) %all-to-all-start.2) | async-done | bytes 544 | tf_op jit(solution)/shard_map/all_to_all | solution.py:105
  389.5 7.6 %all-to-all-start = ((bf16[64,4,3584]{2,1,0:T(4,128)(2,1)}), bf16[64,4,3584]{2,1,0:T(4,128)(2,1)}, u32[]{:S(2)}, u32[]{:S(2)}) async-start(bf16[64,4,3584]{2,1,0:T(4,128)(2,1)} %reshape.107), calls=%async_computation | async-start | bytes 3670016 | tf_op jit(solution)/shard_map/all_to_all | solution.py:98
  397.1 0.4 copy.71
  397.6 0.1 constant_dynamic-slice_fusion.1
  397.7 0.1 copy.72
  397.8 0.1 compare_reduce_fusion.2
  397.9 0.2 reduce_window_sum.28
  398.1 0.3 copy.73
  398.5 0.4 copy.74
  398.9 0.1 constant_dynamic-slice_fusion
  399.0 0.1 copy.75
  399.2 0.1 fusion.30
  399.4 0.2 fusion.33
  399.6 0.7 copy.96
  400.3 152.1 %all-to-all-done = bf16[64,4,3584]{2,1,0:T(4,128)(2,1)} async-done(((bf16[64,4,3584]{2,1,0:T(4,128)(2,1)}), bf16[64,4,3584]{2,1,0:T(4,128)(2,1)}, u32[]{:S(2)}, u32[]{:S(2)}) %all-to-all-start) | async-done | bytes 1835040 | tf_op jit(solution)/shard_map/all_to_all | solution.py:98
  552.4 28.0 %all-to-all-start.3 = ((bf16[16,2,8]{2,1,0:T(2,128)(2,1)}), bf16[16,2,8]{2,1,0:T(2,128)(2,1)S(1)}, u32[]{:S(2)}, u32[]{:S(2)}) async-start(bf16[16,2,8]{2,1,0:T(2,128)(2,1)} %bitcast.29), calls=%async_computation.3 | async-start | bytes 16384 | tf_op jit(solution)/shard_map/all_to_all | solution.py:128
  580.4 2.4 convert_reduce_fusion
  582.8 0.6 fusion.1
  583.5 0.8 reshape.108
  584.2 1.6 all-to-all-done.3
  585.8 4.1 all-to-all-start.1
  589.9 0.5 reduce_sum.65
  590.5 6.4 %all-to-all-done.1 = bf16[16,2,3584]{2,1,0:T(2,128)(2,1)S(1)} async-done(((bf16[16,2,3584]{2,1,0:T(2,128)(2,1)}), bf16[16,2,3584]{2,1,0:T(2,128)(2,1)S(1)}, u32[]{:S(2)}, u32[]{:S(2)}) %all-to-all-start.1) | async-done | bytes 229408 | tf_op jit(solution)/shard_map/all_to_all | solution.py:121
  596.9 0.8 reduce_sum.62
  (26 shorter events, 0.4 us)
Async XLA Ops:
  7.2 358.8 %copy-start = (bf16[1,3584,128]{2,1,0:T(8,128)(2,1)S(1)}, bf16[1,3584,128]{2,1,0:T(8,128)(2,1)}, u32[]{:S(2)}) copy-start(bf16[1,3584,128]{2,1,0:T(8,128)(2,1)} %param.11) | copy-start | bytes 2752516
  7.2 69.6 %copy-start.3 = (bf16[1,256,128]{2,1,0:T(8,128)(2,1)S(1)}, bf16[1,256,128]{2,1,0:T(8,128)(2,1)}, u32[]{:S(2)}) copy-start(bf16[1,256,128]{2,1,0:T(8,128)(2,1)} %param.14) | copy-start | bytes 196612
  7.2 69.7 %copy-start.4 = (bf16[1,256,128]{2,1,0:T(8,128)(2,1)S(1)}, bf16[1,256,128]{2,1,0:T(8,128)(2,1)}, u32[]{:S(2)}) copy-start(bf16[1,256,128]{2,1,0:T(8,128)(2,1)} %param.15) | copy-start | bytes 196612
  7.2 333.7 %all-gather.3.cloned.1.call-start = ((), (), s32[]{:S(2)}) async-start(), calls=%async_computation.4 | async-start | bytes 3727360 | tf_op jit(solution)/shard_map/all_gather | solution.py:82
  349.4 17.3 %copy-start.1 = (bf16[1,3584,128]{2,1,0:T(8,128)(2,1)S(1)}, bf16[1,3584,128]{2,1,0:T(8,128)(2,1)}, u32[]{:S(2)}) copy-start(bf16[1,3584,128]{2,1,0:T(8,128)(2,1)} %param.12) | copy-start | bytes 2752516
  352.6 36.9 %all-to-all-start.2 = ((bf16[64,1,4]{2,1,0:T(2,128)(2,1)}), bf16[64,1,4]{2,1,0:T(2,128)(2,1)S(1)}, u32[]{:S(2)}, u32[]{:S(2)}) async-start(bf16[64,1,4]{2,1,0:T(2,128)(2,1)} %convert_element_type.130), calls=%async_computation.2 | async-start | bytes 65536 | tf_op jit(solution)/shard_map/all_to_all | solution.py:105
  368.6 29.5 %copy-start.2 = (f32[2048,8]{0,1:T(8,128)S(1)}, f32[2048,8]{0,1:T(8,128)}, u32[]{:S(2)}) copy-start(f32[2048,8]{0,1:T(8,128)} %param.10) | copy-start | bytes 196612
  389.5 162.9 %all-to-all-start = ((bf16[64,4,3584]{2,1,0:T(4,128)(2,1)}), bf16[64,4,3584]{2,1,0:T(4,128)(2,1)}, u32[]{:S(2)}, u32[]{:S(2)}) async-start(bf16[64,4,3584]{2,1,0:T(4,128)(2,1)} %reshape.107), calls=%async_computation | async-start | bytes 3670016 | tf_op jit(solution)/shard_map/all_to_all | solution.py:98
  552.4 33.4 %all-to-all-start.3 = ((bf16[16,2,8]{2,1,0:T(2,128)(2,1)}), bf16[16,2,8]{2,1,0:T(2,128)(2,1)S(1)}, u32[]{:S(2)}, u32[]{:S(2)}) async-start(bf16[16,2,8]{2,1,0:T(2,128)(2,1)} %bitcast.29), calls=%async_computation.3 | async-start | bytes 16384 | tf_op jit(solution)/shard_map/all_to_all | solution.py:128
  585.8 11.1 %all-to-all-start.1 = ((bf16[16,2,3584]{2,1,0:T(2,128)(2,1)}), bf16[16,2,3584]{2,1,0:T(2,128)(2,1)S(1)}, u32[]{:S(2)}, u32[]{:S(2)}) async-start(bf16[16,2,3584]{2,1,0:T(2,128)(2,1)} %reshape.108), calls=%async_computation.1 | async-start | bytes 458752 | tf_op jit(solution)/shard_map/all_to_all | solution.py:121
Sparse Core Ops, SparseCore 0:
  76.5 264.3 all-gather.2
where the time goes:
time: 605 us
  waiting for transfers between devices  441 us (73%)
  starting transfers between devices  53.1 us (9%)
  other arithmetic  39.6 us (7%)
  blocking collectives  31.4 us (5%)
  local copies, waits for them, and re-layouts  14.4 us (2%)
  between operations  14.3 us (2%)
  matrix products  11.2 us (2%)
    all_gather x1, waiting for transfers between devices, local(): lax.all_gather(compact, 'local', axis=0, tiled=True)  264 us
    all_to_all x1, waiting for transfers between devices, local(): lax.all_to_all(partial_in.reshape(n_local, capacity, model_width), 'local...  152 us
    reduce_or x2, other arithmetic, slot_tables(): is_named = jnp.any(named_route, axis=1)  34.9 us
    all_gather x1, blocking collectives, local(): grad_rows = lax.all_gather(grad_out, 'group', axis=0, tiled=True)  31.4 us
    all_to_all x1, starting transfers between devices, local(): lax.all_to_all(gate_sum.reshape(n_group, tok_dev, route_count), 'group',...  28 us
    all_to_all x1, waiting for transfers between devices, local(): lax.all_to_all(gate_part.reshape(n_local, capacity), 'local', split_axis=...  16.8 us
    all_to_all x1, starting transfers between devices, local(): lax.all_to_all(gate_part.reshape(n_local, capacity), 'local', split_axis=...  13.3 us
  transfers between devices with their start and end apart: 5, of which 5 were waited for; matrix products, arithmetic and copies ran while one was open for 2% of the time, Pallas kernels for 0%

commit v1 on v0

v1 whole, which is shorter than its diff:
```python
import functools

import jax
import jax.numpy as jnp
from jax import lax
from jax.experimental import pallas as pl
from jax.experimental.pallas import tpu as pltpu
from jax.sharding import PartitionSpec as P

MESH = pl.DeviceIdType.MESH
EXP_GROUP = 8
CAP = 4
LIVE = 8
LANES = 128
F32 = jnp.float32
BF16 = jnp.bfloat16


def iota(shape, dim):
    return lax.broadcasted_iota(jnp.int32, shape, dim)


def one(mask):
    return jnp.where(mask, 1.0, 0.0)


def dot(a, b):
    return jnp.dot(a, b, preferred_element_type=F32)


def dot_nt(a, b):
    return lax.dot_general(a, b, (((1,), (1,)), ((), ())), preferred_element_type=F32)


def split_columns(width, parts):
    tiles = width // LANES
    sizes = [(tiles // parts + (i < tiles % parts)) * LANES for i in range(parts)]
    starts = [sum(sizes[:i]) for i in range(parts)]
    return list(zip(starts, sizes))


def kernel(dims, grad, routes_t, weights_t, s_gate, s_up, w_gate, w_up, w_down, grad_in, grad_gate, *scratch):
    n_group, n_z, n_xh, tok, topk, D, n_split, parts_in, parts_out = dims
    n_local = n_z * n_xh
    plane = n_group * n_xh
    rows_z = n_xh * LIVE
    rows = n_z * rows_z
    cut_in = split_columns(D, parts_in)
    cut_out = split_columns(D + LANES, parts_out)
    it = iter(scratch)
    take = lambda n: [next(it) for _ in range(n)]
    plane_recv, gathered, w_cat, w_dn, f_gate, f_up, f_part, k_mat, w_rep, pick, table, plane_send, final_recv = take(13)
    blocks = take(parts_in)
    mine = take(parts_out)
    from_left = take(parts_out)
    from_right = take(parts_out)
    (own_sem, w_sem, ps_sem, pr_sem, fs_sem, fr_sem, gs_r, gr_r, gs_l, gr_l, ss_r, sr_r, ss_l, sr_l) = take(14)

    g = lax.axis_index("group")
    m = lax.axis_index("local")
    z = m // n_xh
    xh = lax.rem(m, n_xh)
    me = g * n_xh + xh
    right = (g, lax.rem(m + n_xh, n_local))
    left = (g, lax.rem(m + n_local - n_xh, n_local))
    expert = g * EXP_GROUP + m // n_split

    def peer(d):
        p = lax.rem(me + d, plane)
        return p, (p // n_xh, z * n_xh + lax.rem(p, n_xh))

    def zmod(v):
        return lax.rem(v + 2 * n_z, n_z)

    w_copies = [
        pltpu.make_async_copy(w_down, w_dn, w_sem.at[0]),
        pltpu.make_async_copy(w_gate, w_cat.at[:, pl.ds(0, LANES)], w_sem.at[1]),
        pltpu.make_async_copy(w_up, w_cat.at[:, pl.ds(LANES, LANES)], w_sem.at[2]),
    ]
    for copy in w_copies:
        copy.start()
    own = pltpu.make_async_copy(grad, plane_recv.at[me], own_sem.at[0])
    own.start()

    barrier = pltpu.get_barrier_semaphore()
    for d in range(1, plane):
        pl.semaphore_signal(barrier, inc=1, device_id=peer(d)[1], device_id_type=MESH)
    for side in (left, right):
        pl.semaphore_signal(barrier, inc=1, device_id=side, device_id_type=MESH)
    pl.semaphore_wait(barrier, plane + 1)

    def plane_copy(d):
        _, dev = peer(d)
        return pltpu.make_async_remote_copy(
            grad, plane_recv.at[me], ps_sem.at[d], pr_sem.at[me], device_id=dev, device_id_type=MESH
        )

    for d in range(1, plane):
        plane_copy(d).start()

    q_pad = 8
    a_id = lambda shape, dim: iota(shape, dim) // 8
    lane_r, lane_c = iota((LANES, LANES), 0), iota((LANES, LANES), 1)
    pair = one(lane_r // tok == lane_c // tok).astype(BF16)
    earlier = one((lane_r // tok == lane_c // tok) & (lane_r < lane_c)).astype(BF16)
    before = one(lane_c // 8 < lane_r // 8).astype(BF16)
    same = one(lane_c // 8 == lane_r // 8).astype(BF16)

    stacked = jnp.concatenate([routes_t[:, pl.ds(a * LANES, LANES)] for a in range(n_group)], axis=0)
    weight = jnp.concatenate([weights_t[:, pl.ds(a * LANES, LANES)] for a in range(n_group)], axis=0)
    in_group = one(stacked // EXP_GROUP == g)
    is_mine = one(stacked == expert)

    def ordered(hits):
        h = hits.astype(BF16)
        total = dot(h, pair).astype(BF16)
        previous = dot(h, earlier).astype(BF16)
        return dot(before, total) + dot(same, previous), dot(same, h)

    group_pos, group_hit = ordered(in_group)
    slot_pos, mine_hit = ordered(is_mine)
    j_id = lax.rem(lane_r, 8)
    placed = (group_hit > 0.5) & (group_pos == (2 * j_id).astype(F32))
    placed_f = one(placed)
    q_id = lax.rem(lane_c, q_pad)
    spread = one((lane_r == z * n_xh * tok + q_id) & (q_id < n_xh * tok)).astype(BF16)
    sent = dot(placed_f.astype(BF16), spread) * one(lane_r // 8 == lane_c // q_pad)
    folded = sum(sent[a * 8 : a * 8 + 8] for a in range(n_group))
    q8 = lax.rem(iota((8, LANES), 1), q_pad)
    pick_f = jnp.concatenate([jnp.where(q8 // tok == x, folded, 0.0) for x in range(n_xh)], axis=0)
    pick[...] = pick_f

    gathered[...] = jnp.zeros_like(gathered)
    own.wait()
    for d in range(1, plane):
        p, dev = peer(d)
        pltpu.make_async_remote_copy(
            grad, plane_recv.at[p], ps_sem.at[d], pr_sem.at[p], device_id=dev, device_id_type=MESH
        ).wait_recv()
    for a in range(n_group):
        for x in range(n_xh):
            gathered[pl.ds(a * q_pad + x * tok, tok), :] = plane_recv[a * n_xh + x].astype(F32)
    pick_b = pick_f.astype(BF16)
    for (start, size), block in zip(cut_in, blocks):
        block[z] = dot(pick_b, gathered[:, pl.ds(start, size)].astype(BF16)).astype(BF16)

    steps_r, steps_l = n_z // 2, n_z - 1 - n_z // 2

    def gather_copy(side, step, c):
        to_right = side == 0
        which = zmod(z - step) if to_right else zmod(z + step)
        return pltpu.make_async_remote_copy(
            blocks[c].at[which],
            blocks[c].at[which],
            (gs_r if to_right else gs_l).at[step, c],
            (gr_r if to_right else gr_l).at[step, c],
            device_id=right if to_right else left,
            device_id_type=MESH,
        )

    def gather_arrived(side, step, c):
        to_right = side == 0
        which = zmod(z - step - 1) if to_right else zmod(z + step + 1)
        pltpu.make_async_remote_copy(
            blocks[c].at[which],
            blocks[c].at[which],
            (gs_r if to_right else gs_l).at[step, c],
            (gr_r if to_right else gr_l).at[step, c],
            device_id=right if to_right else left,
            device_id_type=MESH,
        ).wait_recv()

    def gather_step(step):
        for c in range(parts_in):
            for side, count in ((0, steps_r), (1, steps_l)):
                if step < count:
                    if step:
                        gather_arrived(side, step - 1, c)
                    gather_copy(side, step, c).start()

    def tables():
        blocks_of = lambda v: [v[a * 8 : a * 8 + 8] for a in range(n_group)]
        fold = lambda v: sum(blocks_of(v))
        parts = [fold(placed_f * one((mine_hit > 0.5) & (slot_pos == float(c)))) for c in range(CAP)]
        for k in range(topk):
            parts.append(
                sum(placed_f[a * 8 : a * 8 + 8] * is_mine[a * 8 + k : a * 8 + k + 1] for a in range(n_group))
            )
        named = is_mine * weight
        w_all = sum(
            placed_f[a * 8 : a * 8 + 8] * jnp.sum(named[a * 8 : a * 8 + 8], axis=0, keepdims=True)
            for a in range(n_group)
        )
        w_hi = w_all.astype(BF16).astype(F32)
        w_mid = (w_all - w_hi).astype(BF16).astype(F32)
        parts += [w_hi, w_mid, w_all - w_hi - w_mid, jnp.zeros((8, LANES), F32)]
        stack = jnp.concatenate(parts, axis=0).astype(BF16)
        row, lane = iota((rows, LANES), 0), iota((rows, LANES), 1)
        expand = one(lane // tok == row // LIVE).astype(BF16)
        spread_out = dot_nt(expand, stack) * one(lax.rem(lane, 8) == lax.rem(row, 8))
        table[...] = spread_out.astype(BF16)

    def factors():
        slots = n_local * CAP
        x_id = lambda n: iota((LANES, n), 0) // 8
        t = table[...]
        to_slot = one(x_id(slots) == lax.rem(iota((LANES, slots), 1), CAP)).astype(BF16)
        to_k = one(x_id(LANES) - CAP == iota((LANES, LANES), 1)).astype(BF16)
        to_k = to_k * one(x_id(LANES) < CAP + topk).astype(BF16)
        to_w = one((x_id(LANES) >= CAP + topk) & (x_id(LANES) < CAP + topk + 3)).astype(BF16)
        k_mat[...] = dot(t, to_k)
        w_rep[...] = dot(t, to_w)
        member = dot(t, to_slot) * one(
            iota((rows, slots), 0) // LIVE == iota((rows, slots), 1) // CAP
        )
        member = member.astype(BF16)
        p = dot(member, s_gate[...])
        q = dot(member, s_up[...])
        sigma = jax.nn.sigmoid(p)
        active = p * sigma
        f_gate[...] = q * sigma * (1.0 + p * (1.0 - sigma))
        f_up[...] = active
        f_part[...] = active * q

    for step in range(steps_r):
        gather_step(step)
        if step == 1:
            tables()
        if step == 2:
            factors()
    for c in range(parts_in):
        gather_arrived(0, steps_r - 1, c)
        gather_arrived(1, steps_l - 1, c)

    for copy in w_copies:
        copy.wait()
    act = sum(
        dot_nt(block[...].reshape(rows, size), w_dn[:, pl.ds(start, size)])
        for (start, size), block in zip(cut_in, blocks)
    )
    part = jnp.sum(f_part[...] * act, axis=1, keepdims=True) * k_mat[...]
    pre = jnp.concatenate([(act * f_gate[...]).astype(BF16), (act * f_up[...]).astype(BF16)], axis=1)
    table[...] = part.astype(BF16)
    f_gate[...] = pre[:, :LANES].astype(F32)
    f_up[...] = pre[:, LANES:].astype(F32)

    tile = 4
    tile_rows = tile * rows_z

    @pl.loop(0, n_z // tile)
    def _(i):
        at = pl.ds(pl.multiple_of(i * tile_rows, tile_rows), tile_rows)
        both = jnp.concatenate([f_gate[at, :].astype(BF16), f_up[at, :].astype(BF16)], axis=1)
        w = w_rep[at, :][:, 0:1]
        for (start, size), out in zip(cut_out, mine):
            end = min(start + size, D)
            value = (dot_nt(both, w_cat[pl.ds(start, end - start), :]) * w).astype(BF16)
            out[pl.ds(i * tile, tile), :, pl.ds(0, end - start)] = value.reshape(tile, rows_z, end - start)
            if start + size > D:
                gate = table[at, :].reshape(tile, rows_z, LANES)
                out[pl.ds(i * tile, tile), :, pl.ds(end - start, LANES)] = gate

    def sum_copy(side, step, c, src):
        to_right = side == 0
        return pltpu.make_async_remote_copy(
            src,
            (from_left if to_right else from_right)[c].at[step],
            (ss_r if to_right else ss_l).at[step, c],
            (sr_r if to_right else sr_l).at[step, c],
            device_id=right if to_right else left,
            device_id_type=MESH,
        )

    def sum_step(step):
        for c in range(parts_out):
            for side, count in ((0, steps_r), (1, steps_l)):
                if step < count:
                    held = (from_left if side == 0 else from_right)[c]
                    which = zmod(z + steps_r - step) if side == 0 else zmod(z - steps_l + step)
                    src = mine[c].at[which]
                    if step:
                        sum_copy(side, step - 1, c, src).wait_recv()
                        src = held.at[step - 1]
                        src[...] = (src[...].astype(F32) + mine[c][which].astype(F32)).astype(BF16)
                    sum_copy(side, step, c, src).start()

    for step in range(steps_r):
        sum_step(step)

    for c, (start, size) in enumerate(cut_out):
        sum_copy(0, steps_r - 1, c, mine[c].at[z]).wait_recv()
        sum_copy(1, steps_l - 1, c, mine[c].at[z]).wait_recv()
        total = mine[c][z].astype(F32) + from_left[c][steps_r - 1].astype(F32) + from_right[c][steps_l - 1].astype(F32)
        back = lax.dot_general(
            pick[...].astype(BF16), total.astype(BF16), (((0,), (0,)), ((), ())), preferred_element_type=F32
        )
        for a in range(n_group):
            for x in range(n_xh):
                at = a * q_pad + x * tok
                plane_send[a * n_xh + x, :, pl.ds(start, size)] = back[at : at + tok].astype(BF16)

    def final_copy(d):
        p, dev = peer(d)
        return pltpu.make_async_remote_copy(
            plane_send.at[p], final_recv.at[me], fs_sem.at[d], fr_sem.at[me], device_id=dev, device_id_type=MESH
        )

    own_final = pltpu.make_async_copy(plane_send.at[me], final_recv.at[me], own_sem.at[1])
    own_final.start()
    for d in range(1, plane):
        final_copy(d).start()

    for d in range(1, plane):
        plane_copy(d).wait_send()
    for step in range(steps_r):
        for side, count in ((0, steps_r), (1, steps_l)):
            if step < count:
                for c in range(parts_in):
                    gather_copy(side, step, c).wait_send()
                for c in range(parts_out):
                    sum_copy(side, step, c, mine[c].at[z]).wait_send()

    own_final.wait()
    for d in range(1, plane):
        p, dev = peer(d)
        pltpu.make_async_remote_copy(
            plane_send.at[p], final_recv.at[p], fs_sem.at[d], fr_sem.at[p], device_id=dev, device_id_type=MESH
        ).wait_recv()
    total = final_recv[0].astype(F32)
    for p in range(1, plane):
        total = total + final_recv[p].astype(F32)
    grad_in[...] = total[:, :D].astype(BF16)
    grad_gate[...] = total[:, D:].astype(BF16)
    for d in range(1, plane):
        final_copy(d).wait_send()


def local(n_group, n_local, grad_out, routes, router_weights, gate_weight, up_weight, down_weight, saved_gate, saved_up):
    tok, D = grad_out.shape
    topk = routes.shape[1]
    hid = saved_gate.shape[2]
    n_xh = 2
    n_z = n_local // n_xh
    n_split = n_local // EXP_GROUP
    parts_in = parts_out = 2
    plane = n_group * n_xh
    rows_z = n_xh * LIVE
    rows = n_z * rows_z
    wide = D + LANES
    cut_in, cut_out = split_columns(D, parts_in), split_columns(wide, parts_out)
    steps_r, steps_l = n_z // 2, n_z - 1 - n_z // 2
    dims = (n_group, n_z, n_xh, tok, topk, D, n_split, parts_in, parts_out)
    vmem = pl.BlockSpec(memory_space=pltpu.VMEM)
    hbm = pl.BlockSpec(memory_space=pl.ANY)
    dma = lambda *shape: pltpu.SemaphoreType.DMA(shape)
    scratch = [
        pltpu.VMEM((plane, tok, D), BF16),
        pltpu.VMEM((n_group * 8, D), F32),
        pltpu.VMEM((D, 2 * hid), BF16),
        pltpu.VMEM((hid, D), BF16),
        pltpu.VMEM((rows, hid), F32),
        pltpu.VMEM((rows, hid), F32),
        pltpu.VMEM((rows, hid), F32),
        pltpu.VMEM((rows, LANES), F32),
        pltpu.VMEM((rows, LANES), F32),
        pltpu.VMEM((rows_z, LANES), F32),
        pltpu.VMEM((rows, LANES), BF16),
        pltpu.VMEM((plane, tok, wide), BF16),
        pltpu.VMEM((plane, tok, wide), BF16),
    ]
    scratch += [pltpu.VMEM((n_z, rows_z, size), BF16) for _, size in cut_in]
    scratch += [pltpu.VMEM((n_z, rows_z, size), BF16) for _, size in cut_out]
    scratch += [pltpu.VMEM((steps_r, rows_z, size), BF16) for _, size in cut_out]
    scratch += [pltpu.VMEM((steps_l, rows_z, size), BF16) for _, size in cut_out]
    scratch += [dma(2), dma(3), dma(plane), dma(plane), dma(plane), dma(plane)]
    scratch += [dma(steps_r, parts_in)] * 2 + [dma(steps_l, parts_in)] * 2
    scratch += [dma(steps_r, parts_out)] * 2 + [dma(steps_l, parts_out)] * 2
    grad_in, gate = pl.pallas_call(
        functools.partial(kernel, dims),
        out_shape=(
            jax.ShapeDtypeStruct((tok, D), BF16),
            jax.ShapeDtypeStruct((tok, LANES), BF16),
        ),
        in_specs=[vmem] * 5 + [hbm] * 3,
        out_specs=(vmem, vmem),
        scratch_shapes=scratch,
        compiler_params=pltpu.CompilerParams(
            collective_id=0, has_side_effects=True, vmem_limit_bytes=56 * 1024 * 1024
        ),
        cost_estimate=pl.CostEstimate(
            flops=6 * rows * D * hid, bytes_accessed=3 * 2 * D * hid, transcendentals=rows * hid
        ),
    )(grad_out, routes.T, router_weights.T, saved_gate[0], saved_up[0], gate_weight[0], up_weight[0], down_weight[0])
    return grad_in, gate[:, :topk]


def solution(mesh):
    rows = P(("group", "local"), None)
    whole = P(("group", "local"), None, None)
    return jax.shard_map(
        functools.partial(local, mesh.shape["group"], mesh.shape["local"]),
        mesh=mesh,
        in_specs=(rows, P(), P(), whole, whole, whole, whole, whole),
        out_specs=(rows, rows),
        check_vma=False,
    )
```

time: 605 us -> 173 us (0.29)
  waiting for transfers between devices: 441 us -> 0 us
  Pallas kernels: 0 us -> 170 us
  starting transfers between devices: 53.1 us -> 0 us
  other arithmetic: 39.6 us -> 0 us
  blocking collectives: 31.4 us -> 0 us
  between operations: 14.3 us -> 0.65 us
  local copies, waits for them, and re-layouts: 14.4 us -> 1.84 us
  matrix products: 11.2 us -> 0 us
    all_gather x1 -> x0, waiting for transfers between devices: 264 us -> none  [local(): lax.all_gather(compact, 'local', axis=0, tiled=True)]
    all_to_all x4 -> x0, waiting for transfers between devices: 177 us -> none  [the longest x1 152 us: local(): lax.all_to_all(partial_in.reshape(n_local, capacity, model_width), 'local...]
    pallas_call x0 -> x1, Pallas kernels: none -> 170 us  [local(): pl.pallas_call(functools.partial(kernel, dims), out_shape=(jax.ShapeDtype...]
    all_to_all x4 -> x0, starting transfers between devices: 53.1 us -> none  [the longest x1 28 us: local(): lax.all_to_all(gate_sum.reshape(n_group, tok_dev, route_count), 'group',...]
    reduce_or x2 -> x0, other arithmetic: 34.9 us -> none  [slot_tables(): is_named = jnp.any(named_route, axis=1)]
    all_gather x1 -> x0, blocking collectives: 31.4 us -> none  [local(): grad_rows = lax.all_gather(grad_out, 'group', axis=0, tiled=True)]
    dot_general x7 -> x0, matrix products: 11.2 us -> none  [the longest x1 4.49 us: local(): jnp.einsum('scj,sjf->scf', slot_matrix, gathered, preferred_element_type=...]
    reshape x3 -> x0, local copies, waits for them, and re-layouts: 8.86 us -> none  [the longest x1 4.14 us: local(): partial_in.reshape(n_local, capacity, model_width)]
  transfers between devices with their start and end apart: 5 -> 0, of which waited for: 5 -> 0; matrix products, arithmetic and copies ran while one was open for 2% -> 0% of each run, Pallas kernels for 0% -> 0%
where the time goes in v1:
time: 173 us
  Pallas kernels  170 us (98%)
  local copies, waits for them, and re-layouts  1.84 us (1%)
    pallas_call x1, Pallas kernels, local(): pl.pallas_call(functools.partial(kernel, dims), out_shape=(jax.ShapeDtype...  170 us

profile of v1, /device:TPU:1, one launch (start us, length us, event | category | flops | bytes accessed | tf_op | source)
XLA Modules:
  0.0 172.8 jit_solution(2737917705160779031)
XLA Ops:
  0.6 170.3 %shard_map.95 = (bf16[2,3584]{1,0:T(2,128)(2,1)}, bf16[2,128]{1,0:T(2,128)(2,1)}) custom-call(bf16[2,3584]{1,0:T(2,128)(2,1)} %grad.1, s32[8,2048]{1,0:T(8,128)} %bitcast.11, f32[8,2048]{1,0:T(8,128)} %bitcast.12, bf16[256,128]{1,0:T(8,128)(2,1)} %bitcast.13, bf16[256,128]{1,0:T(8,128)(2,1)} %bitcast.14, bf16[3584,128]{1,0:T(8,128)(2,1)} %bitcast.8, ...), custom_call_target="tpu_custom_call" | custom-call | flops 1409286144 | bytes 2752512 | tf_op jit(solution)/shard_map/pallas_call | solution.py:378
  170.9 0.0 copy-start
  170.9 1.3 copy.12
  172.3 0.0 copy-done
  172.3 0.5 copy.13
Async XLA Ops:
  170.9 1.3 copy-start

commit v2 on v0

v2 whole, which is shorter than its diff:
```python
import functools

import jax
import jax.numpy as jnp
from jax import lax
from jax.experimental import pallas as pl
from jax.experimental.pallas import tpu as pltpu
from jax.sharding import PartitionSpec as P

MESH = pl.DeviceIdType.MESH
EXP_GROUP = 8
CAP = 4
QUARTERS = 4
LANES = 128
F32 = jnp.float32
BF16 = jnp.bfloat16


def iota(shape, dim):
    return lax.broadcasted_iota(jnp.int32, shape, dim)


def one(mask):
    return jnp.where(mask, 1.0, 0.0)


def dot(a, b):
    return jnp.dot(a, b, preferred_element_type=F32)


def dot_nt(a, b):
    return lax.dot_general(a, b, (((1,), (1,)), ((), ())), preferred_element_type=F32)


def dot_tn(a, b):
    return lax.dot_general(a, b, (((0,), (0,)), ((), ())), preferred_element_type=F32)


def offset_of(n):
    return (n + 1) // 2 if n % 2 else -(n // 2)


def kernel(dims, grad, routes_t, weights_t, s_gate, s_up, w_gate, w_up, w_down, grad_in, grad_gate, *scratch):
    n_group, n_z, n_xh, tok, topk, D = dims
    n_local = n_z * n_xh
    n_block = EXP_GROUP
    line = n_z // n_block
    part = D // QUARTERS
    wide = part + LANES
    tall = QUARTERS * CAP
    rows = n_local * tall
    (
        plane_recv, gathered, w_cat, w_dn, f_gate, f_up, f_part, slots, x_buf, y_buf, pair_sum,
        from_left, from_right, total, closing, home, plane_send, final_recv,
        own_sem, w_sem, ps_sem, pr_sem, fs_sem, fr_sem, far_s, far_r, right_s, left_s, line_r, pair_s, pair_r,
        add_s, add_r, up_s, up_r, down_s, down_r, home_s, home_r,
    ) = scratch

    g = lax.axis_index("group")
    m = lax.axis_index("local")
    z = m // n_xh
    xh = lax.rem(m, n_xh)
    other = 1 - xh
    zb = z // line
    r = lax.rem(z, line)
    right = (g, lax.rem(m + n_xh, n_local))
    left = (g, lax.rem(m + n_local - n_xh, n_local))
    pair = (g, z * n_xh + other)

    def block_at(offset):
        return lax.rem(zb + offset + n_block, n_block)

    def far(offset):
        return (g, (block_at(offset) * line + r) * n_xh + xh)

    def peer(d):
        p = lax.rem(g + d, n_group)
        return p, (p, m)

    def remote(src, dst, send, recv, dev):
        return pltpu.make_async_remote_copy(src, dst, send, recv, device_id=dev, device_id_type=MESH)

    w_copies = []
    for q in range(QUARTERS):
        cols = pl.ds(q * part, part)
        w_copies += [
            pltpu.make_async_copy(w_down.at[:, cols], w_dn.at[pl.ds(q * LANES, LANES), :], w_sem.at[q, 0]),
            pltpu.make_async_copy(w_gate.at[cols, :], w_cat.at[:, pl.ds(2 * q * LANES, LANES)], w_sem.at[q, 1]),
            pltpu.make_async_copy(w_up.at[cols, :], w_cat.at[:, pl.ds((2 * q + 1) * LANES, LANES)], w_sem.at[q, 2]),
        ]
    own = pltpu.make_async_copy(grad, plane_recv.at[g], own_sem.at[0])
    own.start()

    barrier = pltpu.get_barrier_semaphore()
    greeted = [peer(d)[1] for d in range(1, n_group)] + [left, right, pair]
    greeted += [far(offset_of(n)) for n in range(1, n_block)]
    for dev in greeted:
        pl.semaphore_signal(barrier, inc=1, device_id=dev, device_id_type=MESH)
    pl.semaphore_wait(barrier, len(greeted))

    def plane_copy(d):
        return remote(grad, plane_recv.at[g], ps_sem.at[d], pr_sem.at[g], peer(d)[1])

    for d in range(1, n_group):
        plane_copy(d).start()
    for copy in w_copies:
        copy.start()

    lane_r, lane_c = iota((LANES, LANES), 0), iota((LANES, LANES), 1)
    stacked = jnp.concatenate([routes_t[:, pl.ds(a * LANES, LANES)] for a in range(n_group)], axis=0)
    weight = jnp.concatenate([weights_t[:, pl.ds(a * LANES, LANES)] for a in range(n_group)], axis=0)
    t_id = lax.rem(lane_c, 8)
    spread = one((lane_r == m * tok + t_id) & (t_id < tok)).astype(BF16)
    source = one(lane_r // 8 == lane_c // 8)

    def fold(v):
        v = v * source
        return sum(v[a * 8 : a * 8 + 8] for a in range(n_group))

    hi = weight.astype(BF16)
    mid = (weight - hi.astype(F32)).astype(BF16)
    low = (weight - hi.astype(F32) - mid.astype(F32)).astype(BF16)
    own_routes = fold(dot(stacked.astype(F32).astype(BF16), spread))
    own_weights = fold(dot(hi, spread) + dot(mid, spread) + dot(low, spread))
    valid = lax.rem(iota((8, LANES), 1), 8) < tok
    own_routes = jnp.where(valid, own_routes, -1.0)
    first = (g * EXP_GROUP).astype(F32)
    hits, hit_w = [], []
    for e in range(EXP_GROUP):
        same = one(own_routes == first + float(e))
        hits.append(jnp.sum(same, axis=0, keepdims=True))
        hit_w.append(jnp.sum(same * own_weights, axis=0, keepdims=True))
    widen = lambda v: jnp.concatenate([jnp.broadcast_to(t, (tall, LANES)) for t in v], axis=0)
    hit = widen(hits)
    order = dot(hit.astype(BF16), one(lane_r < lane_c).astype(BF16))
    table = hit * one(order == lax.rem(lane_r, CAP).astype(F32))
    quarter = lax.rem(lane_r, tall) // CAP
    slot_weight = jnp.sum(table * widen(hit_w), axis=1, keepdims=True)
    padded = jnp.concatenate([own_routes, jnp.full((LANES - topk, LANES), -1.0, F32)], axis=0)
    slot_routes = dot_nt(table.astype(BF16), padded.astype(BF16))
    which_k = one((slot_routes == first + (lane_r // tall).astype(F32)) & (lane_c < topk))
    tables = [(table * one(quarter == q)).astype(BF16) for q in range(QUARTERS)]

    gathered[...] = jnp.zeros_like(gathered)
    own.wait()
    for d in range(1, n_group):
        p, dev = peer(d)
        remote(grad, plane_recv.at[p], ps_sem.at[d], pr_sem.at[p], dev).wait_recv()
    for a in range(n_group):
        gathered[pl.ds(a * 8, tok), :] = plane_recv[a].astype(F32)
    slot_rows = sum(
        dot(tables[q], gathered[:, pl.ds(q * part, part)].astype(BF16)) for q in range(QUARTERS)
    ).astype(BF16)
    slots[...] = slot_rows.reshape(n_block, tall, part)

    def far_copy(n):
        to = block_at(-offset_of(n))
        return remote(slots.at[to], x_buf.at[xh, n, r], far_s.at[n], far_r.at[n], far(-offset_of(n)))

    for n in range(n_block - 1, 0, -1):
        far_copy(n).start()
    x_buf[xh, 0, r] = slots[zb]

    def along(n, k, to_right):
        at = x_buf.at[xh, n, k]
        if to_right:
            return remote(at, at, right_s.at[n, k], line_r.at[n, k], right)
        return remote(at, at, left_s.at[n, k], line_r.at[n, k], left)

    def across(n, k):
        at = x_buf.at[xh, n, k]
        return remote(at, at, pair_s.at[n, k], pair_r.at[n, k], pair)

    def when(condition, action):
        pl.when(condition)(action)

    def pass_on(n, d, to_right):
        k = r - d if to_right else r + d

        def arrived():
            along(n, k, to_right).wait_recv()
            when(r < line - 1 if to_right else r > 0, lambda: along(n, k, to_right).start())
            across(n, k).start()

        when(r >= d if to_right else r + d <= line - 1, arrived)

    def factors():
        tile = 8 * tall

        @pl.loop(0, rows // tile)
        def _(i):
            row = iota((tile, n_local * CAP), 0) + i * tile
            slot = iota((tile, n_local * CAP), 1)
            n = lax.rem(row // (line * tall), n_block)
            offset = jnp.where(lax.rem(n, 2) == 1, (n + 1) // 2, -(n // 2))
            block = lax.rem(zb + offset + n_block, n_block)
            index = (block * line + lax.rem(row // tall, line)) * n_xh + row // (n_block * line * tall)
            member = one(slot == index * CAP + lax.rem(row, CAP)).astype(BF16)
            p = dot(member, s_gate[...])
            q = dot(member, s_up[...])
            sigma = jax.nn.sigmoid(p)
            active = p * sigma
            at = pl.ds(pl.multiple_of(i * tile, tile), tile)
            f_gate[at, :] = q * sigma * (1.0 + p * (1.0 - sigma))
            f_up[at, :] = active
            f_part[at, :] = active * q

    for step in range(n_block + line - 1):
        if step < n_block:
            if step:
                far_copy(step).wait_recv()
            when(r < line - 1, lambda: along(step, r, True).start())
            when(r > 0, lambda: along(step, r, False).start())
            across(step, r).start()
        if step == 0:
            factors()
        for d in range(1, line):
            if 0 <= step - d < n_block:
                pass_on(step - d, d, True)
                pass_on(step - d, d, False)

    for copy in w_copies:
        copy.wait()

    def compute(half, i):
        tile = 2 * line * tall
        row0 = pl.multiple_of((half * (n_block // 2) + i) * tile, tile)
        at = pl.ds(row0, tile)
        x = x_buf[half, pl.ds(2 * i, 2)].reshape(tile, part)
        each = dot_nt(x, w_dn[...])
        q_id = lax.rem(iota((tile, LANES), 0), tall) // CAP
        mine = sum(jnp.where(q_id == q, each[:, q * LANES : (q + 1) * LANES], 0.0) for q in range(QUARTERS))
        mine = mine.reshape(2 * line, 2, 8, LANES)
        mine = mine[:, 0] + mine[:, 1]
        mine = mine + pltpu.roll(mine, CAP, 1)
        act = jnp.stack([mine, mine], axis=1).reshape(tile, LANES)
        gate = jnp.sum(f_part[at, :] * act, axis=1, keepdims=True)
        gate_hi = gate.astype(BF16).astype(F32)
        gates = jnp.where(q_id == 0, gate_hi, jnp.where(q_id == 1, gate - gate_hi, 0.0)).astype(BF16)
        pre = [(act * f_gate[at, :]).astype(BF16), (act * f_up[at, :]).astype(BF16)]
        zero = jnp.zeros_like(pre[0])
        spread_pre = jnp.concatenate([jnp.where(q_id == q, v, zero) for q in range(QUARTERS) for v in pre], axis=1)
        out = dot_nt(spread_pre, w_cat[...]).astype(BF16)
        y_buf[half, pl.ds(2 * i, 2), :, :, pl.ds(0, part)] = out.reshape(2, line, tall, part)
        y_buf[half, pl.ds(2 * i, 2), :, :, pl.ds(part, LANES)] = gates.reshape(2, line, tall, LANES)

    def add_copy(n):
        return remote(y_buf.at[other, n], pair_sum.at[n], add_s.at[n], add_r.at[n], pair)

    for n in range(n_block):
        for k in range(line):
            at = x_buf.at[other, n, k]
            remote(at, at, pair_s.at[n, k], pair_r.at[n, k], pair).wait_recv()

    @pl.loop(0, n_block // 2)
    def _(j):
        i = n_block // 2 - 1 - j
        compute(other, i)
        add_copy(2 * i + 1).start()
        add_copy(2 * i).start()
        compute(xh, i)

    def sum_copy(n, k, to_right):
        src = y_buf.at[xh, n, k]
        if to_right:
            return remote(src, from_left.at[n, k], up_s.at[n, k], up_r.at[n, k], right)
        return remote(src, from_right.at[n, k], down_s.at[n, k], down_r.at[n, k], left)

    def gather_sum(n, k, sides):
        total[...] = y_buf[xh, n, k].astype(F32) + pair_sum[n, k].astype(F32)
        for to_right in sides:

            def add():
                sum_copy(n, k, to_right).wait_recv()
                total[...] += (from_left if to_right else from_right)[n, k].astype(F32)

            when(r > 0 if to_right else r < line - 1, add)

    def send_sum(step, d, to_right):
        p = step - r if to_right else step - (line - 1 - r)
        n = n_block - 1 - p
        k = r + d if to_right else r - d

        def go():
            gather_sum(n, k, (to_right,))
            y_buf[xh, n, k] = total[...].astype(BF16)
            sum_copy(n, k, to_right).start()

        inside = r + d <= line - 1 if to_right else r >= d
        when(inside & (p >= 0) & (p < n_block), go)

    def home_copy(n):
        return remote(closing.at[n], home.at[zb], home_s.at[n], home_r.at[zb], far(offset_of(n)))

    for step in range(n_block + line - 1):
        if step < n_block:
            add_copy(n_block - 1 - step).wait_recv()
        for d in range(line - 1, 0, -1):
            send_sum(step, d, True)
            send_sum(step, d, False)
        n = n_block - 1 - (step - (line - 1))
        if n < n_block:
            gather_sum(n, r, (True, False))
            if n:
                closing[n] = total[...].astype(BF16)
                home_copy(n).start()
            else:
                home[zb] = total[...].astype(BF16)

    for n in range(1, n_block):
        e = block_at(-offset_of(n))
        remote(closing.at[n], home.at[e], home_s.at[n], home_r.at[e], far(offset_of(n))).wait_recv()

    sums = home[...].reshape(n_block * tall, wide).astype(F32)
    weighted = sums[:, :part] * slot_weight
    w_hi = weighted.astype(BF16)
    w_low = (weighted - w_hi.astype(F32)).astype(BF16)
    for q in range(QUARTERS):
        back = (dot_tn(tables[q], w_hi) + dot_tn(tables[q], w_low)).astype(BF16).astype(F32)
        for a in range(n_group):
            plane_send[a, :, pl.ds(q * part, part)] = back[a * 8 : a * 8 + tok].astype(BF16)
    back = dot_tn(table.astype(BF16), (sums[:, part:] * which_k).astype(BF16))
    for a in range(n_group):
        plane_send[a, :, pl.ds(D, LANES)] = back[a * 8 : a * 8 + tok].astype(BF16)

    def final_copy(d):
        p, dev = peer(d)
        return remote(plane_send.at[p], final_recv.at[g], fs_sem.at[d], fr_sem.at[g], dev)

    own_final = pltpu.make_async_copy(plane_send.at[g], final_recv.at[g], own_sem.at[1])
    own_final.start()
    for d in range(1, n_group):
        final_copy(d).start()

    for d in range(1, n_group):
        plane_copy(d).wait_send()
    for n in range(n_block):
        if n:
            far_copy(n).wait_send()
            home_copy(n).wait_send()
        add_copy(n).wait_send()
        for k in range(line):
            across(n, k).wait_send()
            when((r < line - 1) & (k <= r), lambda: along(n, k, True).wait_send())
            when((r > 0) & (k >= r), lambda: along(n, k, False).wait_send())
            when(k > r, lambda: sum_copy(n, k, True).wait_send())
            when(k < r, lambda: sum_copy(n, k, False).wait_send())

    own_final.wait()
    for d in range(1, n_group):
        p, dev = peer(d)
        remote(plane_send.at[p], final_recv.at[p], fs_sem.at[d], fr_sem.at[p], dev).wait_recv()
    result = final_recv[0].astype(F32)
    for p in range(1, n_group):
        result = result + final_recv[p].astype(F32)
    grad_in[...] = result[:, :D].astype(BF16)
    grad_gate[...] = result[:, D:].astype(BF16)
    for d in range(1, n_group):
        final_copy(d).wait_send()


def local(n_group, n_local, grad_out, routes, router_weights, gate_weight, up_weight, down_weight, saved_gate, saved_up):
    tok, D = grad_out.shape
    topk = routes.shape[1]
    hid = saved_gate.shape[2]
    n_xh = 2
    n_z = n_local // n_xh
    n_block = EXP_GROUP
    line = n_z // n_block
    part = D // QUARTERS
    wide = part + LANES
    tall = QUARTERS * CAP
    rows = n_local * tall
    dims = (n_group, n_z, n_xh, tok, topk, D)
    vmem = pl.BlockSpec(memory_space=pltpu.VMEM)
    hbm = pl.BlockSpec(memory_space=pl.ANY)
    dma = lambda *shape: pltpu.SemaphoreType.DMA(shape)
    scratch = [
        pltpu.VMEM((n_group, tok, D), BF16),
        pltpu.VMEM((n_group * 8, D), F32),
        pltpu.VMEM((part, 2 * QUARTERS * hid), BF16),
        pltpu.VMEM((QUARTERS * hid, part), BF16),
        pltpu.VMEM((rows, hid), F32),
        pltpu.VMEM((rows, hid), F32),
        pltpu.VMEM((rows, hid), F32),
        pltpu.VMEM((n_block, tall, part), BF16),
        pltpu.VMEM((n_xh, n_block, line, tall, part), BF16),
        pltpu.VMEM((n_xh, n_block, line, tall, wide), BF16),
        pltpu.VMEM((n_block, line, tall, wide), BF16),
        pltpu.VMEM((n_block, line, tall, wide), BF16),
        pltpu.VMEM((n_block, line, tall, wide), BF16),
        pltpu.VMEM((tall, wide), F32),
        pltpu.VMEM((n_block, tall, wide), BF16),
        pltpu.VMEM((n_block, tall, wide), BF16),
        pltpu.VMEM((n_group, tok, D + LANES), BF16),
        pltpu.VMEM((n_group, tok, D + LANES), BF16),
    ]
    scratch += [dma(2), dma(QUARTERS, 3)] + [dma(n_group)] * 4 + [dma(n_block)] * 2
    scratch += [dma(n_block, line)] * 5 + [dma(n_block)] * 2 + [dma(n_block, line)] * 4 + [dma(n_block)] * 2
    grad_in, gate = pl.pallas_call(
        functools.partial(kernel, dims),
        out_shape=(
            jax.ShapeDtypeStruct((tok, D), BF16),
            jax.ShapeDtypeStruct((tok, LANES), BF16),
        ),
        in_specs=[vmem] * 5 + [hbm] * 3,
        out_specs=(vmem, vmem),
        scratch_shapes=scratch,
        compiler_params=pltpu.CompilerParams(
            collective_id=0, has_side_effects=True, vmem_limit_bytes=56 * 1024 * 1024
        ),
        cost_estimate=pl.CostEstimate(
            flops=6 * rows * D * hid, bytes_accessed=3 * 2 * D * hid, transcendentals=rows * hid
        ),
    )(grad_out, routes.T, router_weights.T, saved_gate[0], saved_up[0], gate_weight[0], up_weight[0], down_weight[0])
    return grad_in, gate[:, :topk]


def solution(mesh):
    rows = P(("group", "local"), None)
    whole = P(("group", "local"), None, None)
    return jax.shard_map(
        functools.partial(local, mesh.shape["group"], mesh.shape["local"]),
        mesh=mesh,
        in_specs=(rows, P(), P(), whole, whole, whole, whole, whole),
        out_specs=(rows, rows),
        check_vma=False,
    )
```

time: 605 us -> 151 us (0.25)
  waiting for transfers between devices: 441 us -> 0 us
  Pallas kernels: 0 us -> 148 us
  starting transfers between devices: 53.1 us -> 0 us
  other arithmetic: 39.6 us -> 0 us
  blocking collectives: 31.4 us -> 0 us
  between operations: 14.3 us -> 0.65 us
  local copies, waits for them, and re-layouts: 14.4 us -> 1.84 us
  matrix products: 11.2 us -> 0 us
    all_gather x1 -> x0, waiting for transfers between devices: 264 us -> none  [local(): lax.all_gather(compact, 'local', axis=0, tiled=True)]
    all_to_all x4 -> x0, waiting for transfers between devices: 177 us -> none  [the longest x1 152 us: local(): lax.all_to_all(partial_in.reshape(n_local, capacity, model_width), 'local...]
    pallas_call x0 -> x1, Pallas kernels: none -> 148 us  [local(): pl.pallas_call(functools.partial(kernel, dims), out_shape=(jax.ShapeDtype...]
    all_to_all x4 -> x0, starting transfers between devices: 53.1 us -> none  [the longest x1 28 us: local(): lax.all_to_all(gate_sum.reshape(n_group, tok_dev, route_count), 'group',...]
    reduce_or x2 -> x0, other arithmetic: 34.9 us -> none  [slot_tables(): is_named = jnp.any(named_route, axis=1)]
    all_gather x1 -> x0, blocking collectives: 31.4 us -> none  [local(): grad_rows = lax.all_gather(grad_out, 'group', axis=0, tiled=True)]
    dot_general x7 -> x0, matrix products: 11.2 us -> none  [the longest x1 4.49 us: local(): jnp.einsum('scj,sjf->scf', slot_matrix, gathered, preferred_element_type=...]
    reshape x3 -> x0, local copies, waits for them, and re-layouts: 8.86 us -> none  [the longest x1 4.14 us: local(): partial_in.reshape(n_local, capacity, model_width)]
  transfers between devices with their start and end apart: 5 -> 0, of which waited for: 5 -> 0; matrix products, arithmetic and copies ran while one was open for 2% -> 0% of each run, Pallas kernels for 0% -> 0%
where the time goes in v2:
time: 151 us
  Pallas kernels  148 us (98%)
  local copies, waits for them, and re-layouts  1.84 us (1%)
    pallas_call x1, Pallas kernels, local(): pl.pallas_call(functools.partial(kernel, dims), out_shape=(jax.ShapeDtype...  148 us

profile of v2, /device:TPU:1, one launch (start us, length us, event | category | flops | bytes accessed | tf_op | source)
XLA Modules:
  0.0 150.5 jit_solution(1355355001521296682)
XLA Ops:
  0.6 148.0 %shard_map.95 = (bf16[2,3584]{1,0:T(2,128)(2,1)}, bf16[2,128]{1,0:T(2,128)(2,1)}) custom-call(bf16[2,3584]{1,0:T(2,128)(2,1)} %grad.1, s32[8,2048]{1,0:T(8,128)} %bitcast.11, f32[8,2048]{1,0:T(8,128)} %bitcast.12, bf16[256,128]{1,0:T(8,128)(2,1)} %bitcast.13, bf16[256,128]{1,0:T(8,128)(2,1)} %bitcast.14, bf16[3584,128]{1,0:T(8,128)(2,1)} %bitcast.8, ...), custom_call_target="tpu_custom_call" | custom-call | flops 2818572288 | bytes 2752512 | tf_op jit(solution)/shard_map/pallas_call | solution.py:400
  148.7 0.0 copy-start
  148.7 1.3 copy.12
  150.0 0.0 copy-done
  150.0 0.5 copy.13
Async XLA Ops:
  148.7 1.3 copy-start

commit v3 on v2

--- a/solution.py
+++ b/solution.py
@@ -11,6 +11,7 @@
 EXP_GROUP = 8
 CAP = 4
 QUARTERS = 4
+NEAR = 4
 LANES = 128
 F32 = jnp.float32
 BF16 = jnp.bfloat16
@@ -37,7 +38,8 @@
 
 
 def offset_of(n):
-    return (n + 1) // 2 if n % 2 else -(n // 2)
+    half = lax.div(n + 1, 2)
+    return jnp.where(lax.rem(n, 2) == 1, half, -half)
 
 
 def kernel(dims, grad, routes_t, weights_t, s_gate, s_up, w_gate, w_up, w_down, grad_in, grad_gate, *scratch):
@@ -54,6 +56,7 @@
         from_left, from_right, total, closing, home, plane_send, final_recv,
         own_sem, w_sem, ps_sem, pr_sem, fs_sem, fr_sem, far_s, far_r, right_s, left_s, line_r, pair_s, pair_r,
         add_s, add_r, up_s, up_r, down_s, down_r, home_s, home_r,
+        relay_x, relay_h, leg_r, relay_s, home_leg_r, home_relay_s,
     ) = scratch
 
     g = lax.axis_index("group")
@@ -90,21 +93,24 @@
         ]
     own = pltpu.make_async_copy(grad, plane_recv.at[g], own_sem.at[0])
     own.start()
-
-    barrier = pltpu.get_barrier_semaphore()
-    greeted = [peer(d)[1] for d in range(1, n_group)] + [left, right, pair]
-    greeted += [far(offset_of(n)) for n in range(1, n_block)]
-    for dev in greeted:
-        pl.semaphore_signal(barrier, inc=1, device_id=dev, device_id_type=MESH)
-    pl.semaphore_wait(barrier, len(greeted))
-
-    def plane_copy(d):
-        return remote(grad, plane_recv.at[g], ps_sem.at[d], pr_sem.at[g], peer(d)[1])
-
-    for d in range(1, n_group):
-        plane_copy(d).start()
     for copy in w_copies:
         copy.start()
+
+    barrier = pltpu.get_barrier_semaphore()
+
+    def greet(dev):
+        pl.semaphore_signal(barrier, inc=1, device_id=dev, device_id_type=MESH)
+
+    @pl.loop(1, NEAR + 1)
+    def _(n):
+        greet(far(offset_of(n)))
+
+    @pl.loop(1, n_group)
+    def _(d):
+        greet(peer(d)[1])
+
+    for dev in (left, right, pair):
+        greet(dev)
 
     lane_r, lane_c = iota((LANES, LANES), 0), iota((LANES, LANES), 1)
     stacked = jnp.concatenate([routes_t[:, pl.ds(a * LANES, LANES)] for a in range(n_group)], axis=0)
@@ -142,12 +148,47 @@
     tables = [(table * one(quarter == q)).astype(BF16) for q in range(QUARTERS)]
 
     gathered[...] = jnp.zeros_like(gathered)
+
+    f_tile = 8 * tall
+
+    @pl.loop(0, rows // f_tile)
+    def _(i):
+        row = iota((f_tile, n_local * CAP), 0) + i * f_tile
+        slot = iota((f_tile, n_local * CAP), 1)
+        n = lax.rem(row // (line * tall), n_block)
+        block = lax.rem(zb + offset_of(n) + n_block, n_block)
+        index = (block * line + lax.rem(row // tall, line)) * n_xh + row // (n_block * line * tall)
+        member = one(slot == index * CAP + lax.rem(row, CAP)).astype(BF16)
+        p = dot(member, s_gate[...])
+        q = dot(member, s_up[...])
+        sigma = jax.nn.sigmoid(p)
+        active = p * sigma
+        at = pl.ds(pl.multiple_of(i * f_tile, f_tile), f_tile)
+        f_gate[at, :] = q * sigma * (1.0 + p * (1.0 - sigma))
+        f_up[at, :] = active
+        f_part[at, :] = active * q
+
+    pl.semaphore_wait(barrier, NEAR + n_group - 1 + 3)
+
+    def plane_copy(d):
+        return remote(grad, plane_recv.at[g], ps_sem.at[d], pr_sem.at[g], peer(d)[1])
+
+    @pl.loop(1, n_group)
+    def _(d):
+        plane_copy(d).start()
+
+
     own.wait()
-    for d in range(1, n_group):
+
+    @pl.loop(1, n_group)
+    def _(d):
         p, dev = peer(d)
         remote(grad, plane_recv.at[p], ps_sem.at[d], pr_sem.at[p], dev).wait_recv()
-    for a in range(n_group):
-        gathered[pl.ds(a * 8, tok), :] = plane_recv[a].astype(F32)
+
+    @pl.loop(0, n_group)
+    def _(a):
+        gathered[pl.ds(pl.multiple_of(a * 8, 8), tok), :] = plane_recv[a].astype(F32)
+
     slot_rows = sum(
         dot(tables[q], gathered[:, pl.ds(q * part, part)].astype(BF16)) for q in range(QUARTERS)
     ).astype(BF16)
@@ -157,8 +198,20 @@
         to = block_at(-offset_of(n))
         return remote(slots.at[to], x_buf.at[xh, n, r], far_s.at[n], far_r.at[n], far(-offset_of(n)))
 
-    for n in range(n_block - 1, 0, -1):
-        far_copy(n).start()
+    turn = 2 * (1 - 2 * lax.rem(g, 2))
+    first_leg, second_leg = {5: 2, 6: -2, 7: turn}, {5: 1, 6: -1, 7: turn}
+
+    def leg_copy(n):
+        to = block_at(-offset_of(n))
+        at = n - NEAR - 1
+        return remote(slots.at[to], relay_x.at[at], far_s.at[n], leg_r.at[at], far(-first_leg[n]))
+
+    def relay_copy(n):
+        at = n - NEAR - 1
+        return remote(relay_x.at[at], x_buf.at[xh, n, r], relay_s.at[at], far_r.at[n], far(-second_leg[n]))
+
+    for n in (1, 2, 7, 5, 6, 3, 4):
+        (far_copy if n <= NEAR else leg_copy)(n).start()
     x_buf[xh, 0, r] = slots[zb]
 
     def along(n, k, to_right):
@@ -182,55 +235,21 @@
             when(r < line - 1 if to_right else r > 0, lambda: along(n, k, to_right).start())
             across(n, k).start()
 
-        when(r >= d if to_right else r + d <= line - 1, arrived)
-
-    def factors():
-        tile = 8 * tall
-
-        @pl.loop(0, rows // tile)
-        def _(i):
-            row = iota((tile, n_local * CAP), 0) + i * tile
-            slot = iota((tile, n_local * CAP), 1)
-            n = lax.rem(row // (line * tall), n_block)
-            offset = jnp.where(lax.rem(n, 2) == 1, (n + 1) // 2, -(n // 2))
-            block = lax.rem(zb + offset + n_block, n_block)
-            index = (block * line + lax.rem(row // tall, line)) * n_xh + row // (n_block * line * tall)
-            member = one(slot == index * CAP + lax.rem(row, CAP)).astype(BF16)
-            p = dot(member, s_gate[...])
-            q = dot(member, s_up[...])
-            sigma = jax.nn.sigmoid(p)
-            active = p * sigma
-            at = pl.ds(pl.multiple_of(i * tile, tile), tile)
-            f_gate[at, :] = q * sigma * (1.0 + p * (1.0 - sigma))
-            f_up[at, :] = active
-            f_part[at, :] = active * q
-
-    for step in range(n_block + line - 1):
-        if step < n_block:
-            if step:
-                far_copy(step).wait_recv()
-            when(r < line - 1, lambda: along(step, r, True).start())
-            when(r > 0, lambda: along(step, r, False).start())
-            across(step, r).start()
-        if step == 0:
-            factors()
-        for d in range(1, line):
-            if 0 <= step - d < n_block:
-                pass_on(step - d, d, True)
-                pass_on(step - d, d, False)
-
-    for copy in w_copies:
-        copy.wait()
+        inside = r >= d if to_right else r + d <= line - 1
+        when(inside & (n >= 0) & (n < n_block), arrived)
+
+    per = 4
+    n_tile = n_block // per
 
     def compute(half, i):
-        tile = 2 * line * tall
-        row0 = pl.multiple_of((half * (n_block // 2) + i) * tile, tile)
+        tile = per * line * tall
+        row0 = pl.multiple_of((half * n_tile + i) * tile, tile)
         at = pl.ds(row0, tile)
-        x = x_buf[half, pl.ds(2 * i, 2)].reshape(tile, part)
+        x = x_buf[half, pl.ds(per * i, per)].reshape(tile, part)
         each = dot_nt(x, w_dn[...])
         q_id = lax.rem(iota((tile, LANES), 0), tall) // CAP
         mine = sum(jnp.where(q_id == q, each[:, q * LANES : (q + 1) * LANES], 0.0) for q in range(QUARTERS))
-        mine = mine.reshape(2 * line, 2, 8, LANES)
+        mine = mine.reshape(per * line, 2, 8, LANES)
         mine = mine[:, 0] + mine[:, 1]
         mine = mine + pltpu.roll(mine, CAP, 1)
         act = jnp.stack([mine, mine], axis=1).reshape(tile, LANES)
@@ -241,24 +260,53 @@
         zero = jnp.zeros_like(pre[0])
         spread_pre = jnp.concatenate([jnp.where(q_id == q, v, zero) for q in range(QUARTERS) for v in pre], axis=1)
         out = dot_nt(spread_pre, w_cat[...]).astype(BF16)
-        y_buf[half, pl.ds(2 * i, 2), :, :, pl.ds(0, part)] = out.reshape(2, line, tall, part)
-        y_buf[half, pl.ds(2 * i, 2), :, :, pl.ds(part, LANES)] = gates.reshape(2, line, tall, LANES)
+        y_buf[half, pl.ds(per * i, per), :, :, pl.ds(0, part)] = out.reshape(per, line, tall, part)
+        y_buf[half, pl.ds(per * i, per), :, :, pl.ds(part, LANES)] = gates.reshape(per, line, tall, LANES)
 
     def add_copy(n):
         return remote(y_buf.at[other, n], pair_sum.at[n], add_s.at[n], add_r.at[n], pair)
 
-    for n in range(n_block):
-        for k in range(line):
+    def compute_other(i):
+        @pl.loop(0, per * line)
+        def _(j):
+            n, k = per * i + lax.div(j, line), lax.rem(j, line)
             at = x_buf.at[other, n, k]
             remote(at, at, pair_s.at[n, k], pair_r.at[n, k], pair).wait_recv()
 
-    @pl.loop(0, n_block // 2)
+        compute(other, i)
+
+        @pl.loop(0, per)
+        def _(j):
+            add_copy(per * i + per - 1 - j).start()
+
+
+    @pl.loop(0, n_block + line - 1)
+    def _(step):
+        @pl.when(step < n_block)
+        def _():
+            when(step > 0, lambda: far_copy(step).wait_recv())
+
+            @pl.when(step == 3)
+            def _():
+                for n in (7, 5, 6):
+                    leg_copy(n).wait_recv()
+                    relay_copy(n).start()
+
+            when(r < line - 1, lambda: along(step, r, True).start())
+            when(r > 0, lambda: along(step, r, False).start())
+            across(step, r).start()
+
+        for d in range(1, line):
+            pass_on(step - d, d, True)
+            pass_on(step - d, d, False)
+
+    for copy in w_copies:
+        copy.wait()
+
+    @pl.loop(0, n_tile)
     def _(j):
-        i = n_block // 2 - 1 - j
-        compute(other, i)
-        add_copy(2 * i + 1).start()
-        add_copy(2 * i).start()
-        compute(xh, i)
+        compute_other(n_tile - 1 - j)
+        compute(xh, n_tile - 1 - j)
 
     def sum_copy(n, k, to_right):
         src = y_buf.at[xh, n, k]
@@ -289,25 +337,49 @@
         inside = r + d <= line - 1 if to_right else r >= d
         when(inside & (p >= 0) & (p < n_block), go)
 
+    def home_leg(n):
+        at = n - NEAR - 1
+        return remote(closing.at[n], relay_h.at[at], home_s.at[n], home_leg_r.at[at], far(first_leg[n]))
+
+    def home_relay(n):
+        at, origin = n - NEAR - 1, block_at(-first_leg[n])
+        return remote(relay_h.at[at], home.at[origin], home_relay_s.at[at], home_r.at[origin], far(second_leg[n]))
+
     def home_copy(n):
         return remote(closing.at[n], home.at[zb], home_s.at[n], home_r.at[zb], far(offset_of(n)))
 
-    for step in range(n_block + line - 1):
-        if step < n_block:
-            add_copy(n_block - 1 - step).wait_recv()
+    @pl.loop(0, n_block + line - 1)
+    def _(step):
+        for c, due in ((7, 7), (6, 8), (5, 9)):
+
+            @pl.when(step == due)
+            def _():
+                home_leg(c).wait_recv()
+                home_relay(c).start()
+
+        when(step < n_block, lambda: add_copy(n_block - 1 - step).wait_recv())
         for d in range(line - 1, 0, -1):
             send_sum(step, d, True)
             send_sum(step, d, False)
         n = n_block - 1 - (step - (line - 1))
-        if n < n_block:
+
+        @pl.when(n < n_block)
+        def _():
             gather_sum(n, r, (True, False))
-            if n:
+
+            @pl.when(n > 0)
+            def _():
                 closing[n] = total[...].astype(BF16)
-                home_copy(n).start()
-            else:
+                when(n <= NEAR, lambda: home_copy(n).start())
+                for c in first_leg:
+                    when(n == c, lambda: home_leg(c).start())
+
+            @pl.when(n == 0)
+            def _():
                 home[zb] = total[...].astype(BF16)
 
-    for n in range(1, n_block):
+    @pl.loop(1, n_block)
+    def _(n):
         e = block_at(-offset_of(n))
         remote(closing.at[n], home.at[e], home_s.at[n], home_r.at[e], far(offset_of(n))).wait_recv()
 
@@ -316,12 +388,14 @@
     w_hi = weighted.astype(BF16)
     w_low = (weighted - w_hi.astype(F32)).astype(BF16)
     for q in range(QUARTERS):
-        back = (dot_tn(tables[q], w_hi) + dot_tn(tables[q], w_low)).astype(BF16).astype(F32)
-        for a in range(n_group):
-            plane_send[a, :, pl.ds(q * part, part)] = back[a * 8 : a * 8 + tok].astype(BF16)
-    back = dot_tn(table.astype(BF16), (sums[:, part:] * which_k).astype(BF16))
-    for a in range(n_group):
-        plane_send[a, :, pl.ds(D, LANES)] = back[a * 8 : a * 8 + tok].astype(BF16)
+        gathered[:, pl.ds(q * part, part)] = dot_tn(tables[q], w_hi) + dot_tn(tables[q], w_low)
+    f_part[pl.ds(0, n_group * 8), :] = dot_tn(table.astype(BF16), (sums[:, part:] * which_k).astype(BF16))
+
+    @pl.loop(0, n_group)
+    def _(a):
+        at = pl.ds(pl.multiple_of(a * 8, 8), tok)
+        plane_send[a, :, pl.ds(0, D)] = gathered[at, :].astype(BF16)
+        plane_send[a, :, pl.ds(D, LANES)] = f_part[at, :].astype(BF16)
 
     def final_copy(d):
         p, dev = peer(d)
@@ -329,33 +403,50 @@
 
     own_final = pltpu.make_async_copy(plane_send.at[g], final_recv.at[g], own_sem.at[1])
     own_final.start()
-    for d in range(1, n_group):
+
+    @pl.loop(1, n_group)
+    def _(d):
         final_copy(d).start()
 
-    for d in range(1, n_group):
+    @pl.loop(1, n_group)
+    def _(d):
         plane_copy(d).wait_send()
-    for n in range(n_block):
-        if n:
+
+    @pl.loop(0, n_block)
+    def _(n):
+        @pl.when(n > 0)
+        def _():
             far_copy(n).wait_send()
             home_copy(n).wait_send()
+
         add_copy(n).wait_send()
-        for k in range(line):
+
+        @pl.loop(0, line)
+        def _(k):
             across(n, k).wait_send()
             when((r < line - 1) & (k <= r), lambda: along(n, k, True).wait_send())
             when((r > 0) & (k >= r), lambda: along(n, k, False).wait_send())
             when(k > r, lambda: sum_copy(n, k, True).wait_send())
             when(k < r, lambda: sum_copy(n, k, False).wait_send())
 
+    for n in first_leg:
+        relay_copy(n).wait_send()
+        home_relay(n).wait_send()
     own_final.wait()
-    for d in range(1, n_group):
+
+    @pl.loop(1, n_group)
+    def _(d):
         p, dev = peer(d)
         remote(plane_send.at[p], final_recv.at[p], fs_sem.at[d], fr_sem.at[p], dev).wait_recv()
-    result = final_recv[0].astype(F32)
-    for p in range(1, n_group):
-        result = result + final_recv[p].astype(F32)
+
+    result = lax.fori_loop(
+        1, n_group, lambda p, v: v + final_recv[p].astype(F32), final_recv[0].astype(F32)
+    )
     grad_in[...] = result[:, :D].astype(BF16)
     grad_gate[...] = result[:, D:].astype(BF16)
-    for d in range(1, n_group):
+
+    @pl.loop(1, n_group)
+    def _(d):
         final_copy(d).wait_send()
 
 
@@ -397,6 +488,9 @@
     ]
     scratch += [dma(2), dma(QUARTERS, 3)] + [dma(n_group)] * 4 + [dma(n_block)] * 2
     scratch += [dma(n_block, line)] * 5 + [dma(n_block)] * 2 + [dma(n_block, line)] * 4 + [dma(n_block)] * 2
+    n_relay = n_block - 1 - NEAR
+    scratch += [pltpu.VMEM((n_relay, tall, part), BF16), pltpu.VMEM((n_relay, tall, wide), BF16)]
+    scratch += [dma(n_relay)] * 4
     grad_in, gate = pl.pallas_call(
         functools.partial(kernel, dims),
         out_shape=(

time: 151 us -> 141 us (0.934)
  Pallas kernels: 148 us -> 137 us
    pallas_call x1, Pallas kernels: 148 us -> 137 us  [local(): pl.pallas_call(functools.partial(kernel, dims), out_shape=(jax.ShapeDtype...]
where the time goes in v3:
time: 141 us; the launch traced here: 140 us
  Pallas kernels  137 us (97%)
  local copies, waits for them, and re-layouts  1.84 us (1%)
    pallas_call x1, Pallas kernels, local(): pl.pallas_call(functools.partial(kernel, dims), out_shape=(jax.ShapeDtype...  137 us

profile of v3, /device:TPU:1, one launch (start us, length us, event | category | flops | bytes accessed | tf_op | source)
XLA Modules:
  0.0 139.5 jit_solution(5735570448038739367)
XLA Ops:
  0.6 137.0 %shard_map.95 = (bf16[2,3584]{1,0:T(2,128)(2,1)}, bf16[2,128]{1,0:T(2,128)(2,1)}) custom-call(bf16[2,3584]{1,0:T(2,128)(2,1)} %grad.1, s32[8,2048]{1,0:T(8,128)} %bitcast.11, f32[8,2048]{1,0:T(8,128)} %bitcast.12, bf16[256,128]{1,0:T(8,128)(2,1)} %bitcast.13, bf16[256,128]{1,0:T(8,128)(2,1)} %bitcast.14, bf16[3584,128]{1,0:T(8,128)(2,1)} %bitcast.8, ...), custom_call_target="tpu_custom_call" | custom-call | flops 2818572288 | bytes 2752512 | tf_op jit(solution)/shard_map/pallas_call | solution.py:494
  137.7 0.0 copy-start
  137.7 1.3 copy.12
  139.0 0.0 copy-done
  139.0 0.5 copy.13
Async XLA Ops:
  137.7 1.3 copy-start

commit v4 on v3

--- a/solution.py
+++ b/solution.py
@@ -57,8 +57,17 @@
         own_sem, w_sem, ps_sem, pr_sem, fs_sem, fr_sem, far_s, far_r, right_s, left_s, line_r, pair_s, pair_r,
         add_s, add_r, up_s, up_r, down_s, down_r, home_s, home_r,
         relay_x, relay_h, leg_r, relay_s, home_leg_r, home_relay_s,
+        routes_v, weights_v, s_gate_v, s_up_v, small_sem,
     ) = scratch
 
+    small = [
+        pltpu.make_async_copy(src, dst, small_sem.at[i])
+        for i, (src, dst) in enumerate(
+            [(routes_t, routes_v), (weights_t, weights_v), (s_gate, s_gate_v), (s_up, s_up_v)]
+        )
+    ]
+    for copy in small:
+        copy.start()
     g = lax.axis_index("group")
     m = lax.axis_index("local")
     z = m // n_xh
@@ -112,9 +121,12 @@
     for dev in (left, right, pair):
         greet(dev)
 
+    for copy in small:
+        copy.wait()
+
     lane_r, lane_c = iota((LANES, LANES), 0), iota((LANES, LANES), 1)
-    stacked = jnp.concatenate([routes_t[:, pl.ds(a * LANES, LANES)] for a in range(n_group)], axis=0)
-    weight = jnp.concatenate([weights_t[:, pl.ds(a * LANES, LANES)] for a in range(n_group)], axis=0)
+    stacked = jnp.concatenate([routes_v[:, pl.ds(a * LANES, LANES)] for a in range(n_group)], axis=0)
+    weight = jnp.concatenate([weights_v[:, pl.ds(a * LANES, LANES)] for a in range(n_group)], axis=0)
     t_id = lax.rem(lane_c, 8)
     spread = one((lane_r == m * tok + t_id) & (t_id < tok)).astype(BF16)
     source = one(lane_r // 8 == lane_c // 8)
@@ -159,8 +171,8 @@
         block = lax.rem(zb + offset_of(n) + n_block, n_block)
         index = (block * line + lax.rem(row // tall, line)) * n_xh + row // (n_block * line * tall)
         member = one(slot == index * CAP + lax.rem(row, CAP)).astype(BF16)
-        p = dot(member, s_gate[...])
-        q = dot(member, s_up[...])
+        p = dot(member, s_gate_v[...])
+        q = dot(member, s_up_v[...])
         sigma = jax.nn.sigmoid(p)
         active = p * sigma
         at = pl.ds(pl.multiple_of(i * f_tile, f_tile), f_tile)
@@ -280,7 +292,7 @@
             add_copy(per * i + per - 1 - j).start()
 
 
-    @pl.loop(0, n_block + line - 1)
+    @pl.loop(0, n_block + 2 * line - 2)
     def _(step):
         @pl.when(step < n_block)
         def _():
@@ -297,8 +309,8 @@
             across(step, r).start()
 
         for d in range(1, line):
-            pass_on(step - d, d, True)
-            pass_on(step - d, d, False)
+            pass_on(step - 2 * d, d, True)
+            pass_on(step - 2 * d, d, False)
 
     for copy in w_copies:
         copy.wait()
@@ -491,13 +503,15 @@
     n_relay = n_block - 1 - NEAR
     scratch += [pltpu.VMEM((n_relay, tall, part), BF16), pltpu.VMEM((n_relay, tall, wide), BF16)]
     scratch += [dma(n_relay)] * 4
+    scratch += [pltpu.VMEM((topk, routes.shape[0]), jnp.int32), pltpu.VMEM((topk, routes.shape[0]), F32)]
+    scratch += [pltpu.VMEM(saved_gate.shape[1:], BF16)] * 2 + [dma(4)]
     grad_in, gate = pl.pallas_call(
         functools.partial(kernel, dims),
         out_shape=(
             jax.ShapeDtypeStruct((tok, D), BF16),
             jax.ShapeDtypeStruct((tok, LANES), BF16),
         ),
-        in_specs=[vmem] * 5 + [hbm] * 3,
+        in_specs=[vmem] + [hbm] * 7,
         out_specs=(vmem, vmem),
         scratch_shapes=scratch,
         compiler_params=pltpu.CompilerParams(

time: 141 us -> 136 us (0.965); the launches traced: 140 us -> 136 us
  Pallas kernels: 137 us -> 134 us
    pallas_call x1, Pallas kernels: 137 us -> 134 us  [local(): pl.pallas_call(functools.partial(kernel, dims), out_shape=(jax.ShapeDtype...]
where the time goes in v4:
time: 136 us
  Pallas kernels  134 us (99%)
  local copies, waits for them, and re-layouts  1.84 us (1%)
    pallas_call x1, Pallas kernels, local(): pl.pallas_call(functools.partial(kernel, dims), out_shape=(jax.ShapeDtype...  134 us

profile of v4, /device:TPU:1, one launch (start us, length us, event | category | flops | bytes accessed | tf_op | source)
XLA Modules:
  0.0 136.1 jit_solution(14905262373266945918)
XLA Ops:
  0.6 133.6 %shard_map.95 = (bf16[2,3584]{1,0:T(2,128)(2,1)}, bf16[2,128]{1,0:T(2,128)(2,1)}) custom-call(bf16[2,3584]{1,0:T(2,128)(2,1)} %grad.1, s32[8,2048]{1,0:T(8,128)} %bitcast.11, f32[8,2048]{1,0:T(8,128)} %bitcast.12, bf16[256,128]{1,0:T(8,128)(2,1)} %bitcast.13, bf16[256,128]{1,0:T(8,128)(2,1)} %bitcast.14, bf16[3584,128]{1,0:T(8,128)(2,1)} %bitcast.8, ...), custom_call_target="tpu_custom_call" | custom-call | flops 2818572288 | bytes 2752512 | tf_op jit(solution)/shard_map/pallas_call | solution.py:508
  134.2 0.0 copy-start
  134.2 1.3 copy.12
  135.6 0.0 copy-done
  135.6 0.5 copy.13
Async XLA Ops:
  134.2 1.3 copy-start
